TPU v7x, 512 devices: a whole 4x8x8 slice. The times are simulated.
512 devices in a mesh: bank: 128 (over y, z, x_hi), tm: 4 (over x_lo, core).
Axes of the slice: x: 4 (x_hi: 2, x_lo: 2; x = x_hi * 2 + x_lo), y: 8, z: 8, core: 2. Of those that a mesh axis runs over, the one named last changes fastest.
Arguments:
- strain: float32 [3, 4, 16384], P(None, 'tm', 'bank'), may hold values from -6 to 6
- fir_taps: float32 [4096], replicated, may hold values from -0.09375 to 0.09375
- templates: bfloat16 [256, 2, 2048], P('bank'), may hold values from -6 to 6
Outputs:
- snr_sq: float32 [3, 256, 65536], P(None, 'bank', 'tm')
- loudest: float32 [3, 65536], P(None, 'tm')
All inputs are finite; a program needn't handle non-finite values.
Results may differ from a plain program's by a relative error of at most 0.003.
Values may be sent and summed in bfloat16 or wider, within the bound.
A program may use at most 64 MiB of HBM per device.

v0:
```python
import jax
import jax.numpy as jnp
from jax import lax
from jax.sharding import PartitionSpec as P


def with_halo(block, sides, width):
    for axis, dim in sides:
        count = lax.axis_size(axis)
        forward = [(i, i + 1) for i in range(count - 1)]
        forward.append((count - 1, 0))
        backward = [(target, source) for source, target in forward]
        low = lax.ppermute(
            lax.slice_in_dim(block, block.shape[dim] - width, None, axis=dim), axis, forward
        )
        high = lax.ppermute(lax.slice_in_dim(block, 0, width, axis=dim), axis, backward)
        block = jnp.concatenate([low, block, high], axis=dim)
    return block


def toeplitz_table(filt, reach_count):
    filters, span_len = filt.shape
    lane_count = 128
    cycle_len = lane_count * reach_count + lane_count
    padded_filt = jnp.pad(filt, ((0, 0), (0, cycle_len - span_len)))
    tiled = jnp.tile(padded_filt, (1, lane_count))[:, : lane_count * (cycle_len - 1)]
    return tiled.reshape(filters, lane_count, cycle_len - 1)[:, :, : lane_count * reach_count]


def slide(signals, table, span_len, precision):
    row_count, length = signals.shape
    filters = table.shape[0]
    lane_count = 128
    reach_count = table.shape[2] // lane_count
    out_len = length - span_len + 1
    frames = (out_len + lane_count - 1) // lane_count
    full_len = lane_count * (frames + reach_count)
    signals = jnp.pad(signals, ((0, 0), (0, full_len - length)))
    framed = signals.reshape(row_count, frames + reach_count, lane_count)
    windows = jnp.concatenate(
        [framed[:, offset : offset + frames] for offset in range(reach_count)], axis=2
    )
    result = lax.dot_general(
        windows,
        table,
        (((2,), (2,)), ((), ())),
        preferred_element_type=jnp.float32,
        precision=precision,
    )
    result = jnp.transpose(result, (0, 2, 1, 3)).reshape(row_count, filters, frames * lane_count)
    return result[:, :, :out_len]


def reach_of(span_len):
    return (span_len + 127 + 127) // 128


def whiten_rows(signal, fir_taps):
    tap_count = fir_taps.shape[0]
    table = toeplitz_table(fir_taps.reshape(1, tap_count), reach_of(tap_count))
    return slide(signal, table, tap_count, lax.Precision.HIGHEST)[:, 0, :]


def shards(strain, fir_taps, templates):
    stretch_part = strain[:, 0, :]
    gathered = lax.all_gather(stretch_part, "bank", axis=1, tiled=True)
    stretch_len = gathered.shape[1]
    tmpl_len = templates.shape[2]
    tap_count = fir_taps.shape[0]
    margin = tap_count // 2 + tmpl_len // 2
    extended = with_halo(gathered, (("tm", 1),), margin)
    white_len = stretch_len + tmpl_len - 1
    whitened = whiten_rows(extended[:, : white_len + tap_count - 1], fir_taps).astype(jnp.bfloat16)
    tmpl_dev = templates.shape[0]
    bank_rows = templates.reshape(tmpl_dev * 2, tmpl_len)
    bank_table = toeplitz_table(bank_rows, reach_of(tmpl_len))
    energy = jnp.mean(jnp.square(templates.astype(jnp.float32)), axis=(1, 2)) + 1e-06
    divisor = tmpl_len * energy
    result = slide(whitened, bank_table, tmpl_len, None)
    result = result.reshape(whitened.shape[0], tmpl_dev, 2, stretch_len)
    snr_sq = jnp.sum(result * result, axis=2) / divisor[None, :, None]
    top_power = lax.pmax(jnp.max(snr_sq, axis=1), "bank")
    return (snr_sq, top_power)


def solution(mesh):
    in_specs = (P(None, "tm", "bank"), P(), P("bank", None, None))
    out_specs = (P(None, "bank", "tm"), P(None, "tm"))
    return jax.shard_map(shards, mesh=mesh, in_specs=in_specs, out_specs=out_specs, check_vma=False)
```

profile of v0, /device:TPU:16, one launch (start us, length us, event | category | flops | bytes accessed | tf_op | source)
XLA Modules:
  0.0 1681.6 jit_solution(14929333578318406595)
XLA Ops:
  7.2 0.0 all-reduce.6.cloned.1.call-start
  7.2 321.0 %all-gather = f32[3,1,16384]{2,1,0:T(1,128)S(1)} all-gather(f32[3,1,128]{2,1,0:T(1,128)} %param.3), channel_id=2, replica_groups=mesh['bank'=128,'tm'=4] {'bank'}, dimensions={2}, use_global_device_ids=true | all-gather | bytes 198144 | tf_op jit(solution)/shard_map/all_gather | solution.py:66
  328.2 0.1 copy.10
  328.3 1.9 collective-permute-start
  330.3 3.6 collective-permute-start.1
  333.9 0.7 reshape.49
  334.6 0.8 multiply_reduce_fusion
  335.5 0.8 pad_reduce_fusion
  336.2 0.1 broadcast_bitcast_fusion.1
  336.4 2.3 copy.7
  338.7 24.4 %slice_reduce_fusion = f32[556928]{0:T(1024)} fusion(f32[1,557056]{1,0:T(1,128)S(1)} %bitcast.41), kind=kLoop, calls=%fused_computation.2 | loop fusion | bytes 4455424 | tf_op jit(solution)/shard_map/slice | solution.py:26
  363.1 0.2 broadcast_bitcast_fusion
  363.3 4.5 reshape.46
  367.8 1.8 copy.8
  369.7 2.3 slice.288
  372.0 3.3 reshape.57
  375.3 6.0 reshape.50
  381.3 0.0 collective-permute-done
  381.3 0.1 select_maximum_fusion
  381.4 0.1 reshape.44
  382.4 0.7 copy-done
  383.1 6.2 fusion.9
  389.4 0.1 slice_bitcast_fusion.10
  389.5 0.1 pad.18
  389.6 0.1 reshape.48
  390.5 1.1 fusion.6
  391.6 0.5 mul.18
  392.1 1.2 reduce_sum.18
  393.3 1.8 fusion.10
  395.1 0.0 all-reduce.6.cloned.1.call-update
  395.1 1277.9 %all-reduce.6.cloned.1.call-done = f32[3,16384]{1,0:T(4,128)} async-done(((f32[3,16384]{1,0:T(4,128)}), f32[3,16384]{1,0:T(4,128)}) %all-reduce.6.cloned.1.call-update) | async-done | bytes 196624 | tf_op jit(solution)/shard_map/pmax | solution.py:82
  1673.0 1.7 copy.60
  (58 shorter events, 1.4 us)
Async XLA Ops:
  7.2 1665.9 %all-reduce.6.cloned.1.call-start = ((), (), s32[]{:S(2)}) async-start(), calls=%async_computation | async-start | bytes 524288 | tf_op jit(solution)/shard_map/pmax | solution.py:82
  328.3 52.9 %collective-permute-start = (f32[3,3072]{1,0:T(4,128)S(1)}, f32[3,3072]{1,0:T(4,128)S(1)}, u32[]{:S(2)}, u32[]{:S(2)}) collective-permute-start(f32[3,3072]{1,0:T(4,128)S(1)} %get-tuple-element.4), channel_id=1, source_target_pairs={{0,1},{1,2},{2,3},{3,0},{4,5},{5,6},{6,7},{7,4},{8,9},{9,10},{10,1... | collective-permute-start | bytes 110600 | tf_op jit(solution)/shard_map/ppermute | solution.py:13
  330.3 51.0 %collective-permute-start.1 = (f32[3,3072]{1,0:T(4,128)S(1)}, f32[3,3072]{1,0:T(4,128)S(1)}, u32[]{:S(2)}, u32[]{:S(2)}) collective-permute-start(f32[3,3072]{1,0:T(4,128)S(1)} %get-tuple-element.5), channel_id=1, source_target_pairs={{1,0},{2,1},{3,2},{0,3},{5,4},{6,5},{7,6},{4,7},{9,8},{10,9},{11,1... | collective-permute-start | bytes 110600 | tf_op jit(solution)/shard_map/ppermute | solution.py:16
  381.5 1.6 copy-start
  382.4 8.1 copy-start.1
Sparse Core Ops, SparseCore 0:
  395.3 1277.7 all-reduce.5
where the time goes:
time: 1680 us
  waiting for transfers between devices  1280 us (76%)
  blocking collectives  321 us (19%)
  local copies, waits for them, and re-layouts  51.3 us (3%)
    pmax x1, waiting for transfers between devices, shards(): top_power = lax.pmax(jnp.max(snr_sq, axis=1), 'bank')  1280 us
    all_gather x1, blocking collectives, shards(): gathered = lax.all_gather(stretch_part, 'bank', axis=1, tiled=True)  321 us
  transfers between devices with their start and end apart: 3, of which 1 were waited for; matrix products, arithmetic and copies ran while one was open for 3% of the time, Pallas kernels for 0%

commit v1 on v0

--- a/solution.py
+++ b/solution.py
@@ -63,7 +63,9 @@
 
 def shards(strain, fir_taps, templates):
     stretch_part = strain[:, 0, :]
-    gathered = lax.all_gather(stretch_part, "bank", axis=1, tiled=True)
+    gathered = jnp.concatenate(
+        lax.all_to_all(jnp.stack([stretch_part] * lax.axis_size("bank")), "bank", 0, 0), axis=1
+    )
     stretch_len = gathered.shape[1]
     tmpl_len = templates.shape[2]
     tap_count = fir_taps.shape[0]

time: 1680 us -> 1350 us (0.80)
  blocking collectives: 321 us -> 0 us
  waiting for transfers between devices: 1280 us -> 1250 us
  starting transfers between devices: 5.6 us -> 25.6 us
    all_gather x1 -> x0, blocking collectives: 321 us -> none  [shards(): gathered = lax.all_gather(stretch_part, 'bank', axis=1, tiled=True)]
    pmax x1, waiting for transfers between devices: 1280 us -> 1250 us  [shards(): top_power = lax.pmax(jnp.max(snr_sq, axis=1), 'bank')]
    all_to_all x0 -> x1, starting transfers between devices: none -> 19.8 us  [shards(): lax.all_to_all(jnp.stack([stretch_part] * lax.axis_size('bank')), 'bank',...]
  transfers between devices with their start and end apart: 3 -> 4, of which waited for: 1 -> 1; matrix products, arithmetic and copies ran while one was open for 3% -> 4% of each run, Pallas kernels for 0% -> 0%
where the time goes in v1:
time: 1350 us
  waiting for transfers between devices  1250 us (93%)
  local copies, waits for them, and re-layouts  55.6 us (4%)
  starting transfers between devices  25.6 us (2%)
  between operations  14.5 us (1%)
    pmax x1, waiting for transfers between devices, shards(): top_power = lax.pmax(jnp.max(snr_sq, axis=1), 'bank')  1250 us
  transfers between devices with their start and end apart: 4, of which 1 were waited for; matrix products, arithmetic and copies ran while one was open for 4% of the time, Pallas kernels for 0%

profile of v1, /device:TPU:16, one launch (start us, length us, event | category | flops | bytes accessed | tf_op | source)
XLA Modules:
  0.0 1353.4 jit_solution(14411016516223254884)
XLA Ops:
  7.2 0.7 copy.10
  7.8 0.7 stack.3
  8.6 19.8 %all-to-all-start = ((f32[128,3,128]{2,1,0:T(4,128)}), f32[128,3,128]{2,1,0:T(4,128)S(1)}, u32[]{:S(2)}, u32[]{:S(2)}) async-start(f32[128,3,128]{2,1,0:T(4,128)} %stack.3), calls=%async_computation | async-start | bytes 524288 | tf_op jit(solution)/shard_map/all_to_all | solution.py:67
  28.4 0.0 all-reduce.6.cloned.1.call-start
  28.5 0.8 pad_reduce_fusion
  29.2 1.5 broadcast_bitcast_fusion.1
  30.7 0.7 reshape.59
  31.5 0.2 broadcast_bitcast_fusion
  31.7 0.8 multiply_reduce_fusion
  32.5 3.9 copy.7
  36.4 24.4 %slice_reduce_fusion = f32[556928]{0:T(1024)} fusion(f32[1,557056]{1,0:T(1,128)S(1)} %bitcast.44), kind=kLoop, calls=%fused_computation.2 | loop fusion | bytes 4455424 | tf_op jit(solution)/shard_map/slice | solution.py:26
  60.9 1.9 collective-permute-start
  62.8 3.8 collective-permute-start.1
  66.6 4.5 reshape.56
  71.2 1.8 copy.8
  73.0 2.3 slice.288
  75.3 3.3 reshape.66
  78.6 6.0 reshape.60
  84.6 0.1 select_maximum_fusion
  84.7 0.1 reshape.54
  85.7 0.7 copy-done
  86.5 6.2 fusion.9
  92.8 0.1 slice_bitcast_fusion.10
  92.8 0.1 pad.18
  92.9 0.1 reshape.58
  93.8 1.1 fusion.6
  94.9 0.5 mul.18
  95.4 1.2 reduce_sum.18
  96.6 1.8 fusion.10
  98.4 0.0 all-reduce.6.cloned.1.call-update
  98.5 1246.4 %all-reduce.6.cloned.1.call-done = f32[3,16384]{1,0:T(4,128)} async-done(((f32[3,16384]{1,0:T(4,128)}), f32[3,16384]{1,0:T(4,128)}) %all-reduce.6.cloned.1.call-update) | async-done | bytes 196624 | tf_op jit(solution)/shard_map/pmax | solution.py:84
  1344.9 1.7 copy.60
  (60 shorter events, 1.4 us)
Async XLA Ops:
  8.6 52.3 %all-to-all-start = ((f32[128,3,128]{2,1,0:T(4,128)}), f32[128,3,128]{2,1,0:T(4,128)S(1)}, u32[]{:S(2)}, u32[]{:S(2)}) async-start(f32[128,3,128]{2,1,0:T(4,128)} %stack.3), calls=%async_computation | async-start | bytes 524288 | tf_op jit(solution)/shard_map/all_to_all | solution.py:67
  28.4 1316.4 %all-reduce.6.cloned.1.call-start = ((), (), s32[]{:S(2)}) async-start(), calls=%async_computation.1 | async-start | bytes 524288 | tf_op jit(solution)/shard_map/pmax | solution.py:84
  60.9 23.7 %collective-permute-start = (f32[3,3072]{1,0:T(4,128)S(1)}, f32[3,3072]{1,0:T(4,128)S(1)}, u32[]{:S(2)}, u32[]{:S(2)}) collective-permute-start(f32[3,3072]{1,0:T(4,128)S(1)} %get-tuple-element.4), channel_id=1, source_target_pairs={{0,1},{1,2},{2,3},{3,0},{4,5},{5,6},{6,7},{7,4},{8,9},{9,10},{10,1... | collective-permute-start | bytes 110600 | tf_op jit(solution)/shard_map/ppermute | solution.py:13
  62.8 21.8 %collective-permute-start.1 = (f32[3,3072]{1,0:T(4,128)S(1)}, f32[3,3072]{1,0:T(4,128)S(1)}, u32[]{:S(2)}, u32[]{:S(2)}) collective-permute-start(f32[3,3072]{1,0:T(4,128)S(1)} %get-tuple-element.5), channel_id=1, source_target_pairs={{1,0},{2,1},{3,2},{0,3},{5,4},{6,5},{7,6},{4,7},{9,8},{10,9},{11,1... | collective-permute-start | bytes 110600 | tf_op jit(solution)/shard_map/ppermute | solution.py:16
  84.8 1.6 copy-start
  85.7 8.1 copy-start.1
Sparse Core Ops, SparseCore 0:
  98.6 1246.2 all-reduce.5
